TPU v7x, 256 devices: a whole 4x4x8 slice. The times are simulated.
256 devices in a mesh: row: 16 (over z_lo, x, core), col: 16 (over y, z_hi).
Axes of the slice: x: 4, y: 4, z: 8 (z_hi: 4, z_lo: 2; z = z_hi * 2 + z_lo), core: 2. Of those that a mesh axis runs over, the one named last changes fastest.
Arguments:
- pair_density: bfloat16 [4096, 8192], P('col', 'row'), may hold values from -6 to 6
- scale_exp: int32 [4096], replicated, may hold values from -1 to 1
- pair_weight: int32 [4096], replicated, may hold values from 1 to 4
- resident_ids: int32 [512], replicated, may hold values from 0 to 4095, as said below
- diagonal_shift: float32 [8192], replicated, may hold values from 2 to 4
- background: float32 [8192, 8192], P('row', 'col'), as said below
Outputs:
- dielectric: float32 [8192, 8192], P('row', 'col')
- kernel: float32 [4096, 512], P(('col', 'row'))
Inputs may be any that keep to these rules, and one draw needn't show every extreme that they name: `resident_ids`: 512 distinct pair indices. background is symmetric.
All inputs are finite; a program needn't handle non-finite values.
Results may differ from a plain program's by a relative error of at most 0.0003.
Values may be sent and summed in bfloat16 or wider, within the bound.
A program may use at most 64 MiB of HBM per device.

v0:
```python
import math
import jax
import jax.numpy as jnp
from jax import lax
from jax.sharding import PartitionSpec as P

NG = 8192
SWEEPS = 2
damping = 0.5


def from_root(block, axis, owner):
    block = jnp.where(lax.axis_index(axis) == owner, block, jnp.zeros_like(block))
    return lax.psum(block, axis)


def scale_factor(exponent):
    return jnp.where(exponent < 0, 0.5, jnp.where(exponent > 0, 2.0, 1.0)).astype(jnp.float32)


def pair_contract(left_block, right_block):
    return lax.dot_general(
        left_block, right_block, (((0,), (0,)), ((), ())), preferred_element_type=jnp.float32
    )


def shards(pair_density, scale_exp, pair_weight, resident_ids, diagonal_shift, background):
    row_count = lax.axis_size("row")
    col_count = lax.axis_size("col")
    row_index = lax.axis_index("row")
    col_index = lax.axis_index("col")
    pair_dev, row_width = pair_density.shape
    col_width = background.shape[1]
    pair_total = pair_dev * col_count
    norm_scale = 4 * pair_total
    factor = scale_factor(scale_exp)
    own_factor = lax.dynamic_slice_in_dim(factor, col_index * pair_dev, pair_dev)
    scaled = (pair_density.astype(jnp.float32) * own_factor[:, None]).astype(jnp.bfloat16)
    left_all = lax.all_gather(scaled, "col", axis=0, tiled=True)
    pair_rows_all = lax.all_gather(scaled, "row", axis=1, tiled=True)
    right_all = lax.all_to_all(pair_rows_all, "col", split_axis=1, concat_axis=0, tiled=True)
    contracted = pair_contract(left_all, right_all)
    response = contracted / norm_scale
    row_start = row_index * row_width
    col_start = col_index * col_width
    global_rows = row_start + lax.broadcasted_iota(jnp.int32, (row_width, col_width), 0)
    global_cols = col_start + lax.broadcasted_iota(jnp.int32, (row_width, col_width), 1)
    shift_rows = lax.dynamic_slice_in_dim(diagonal_shift, row_start, row_width)
    dielectric = (
        background + response + jnp.where(global_rows == global_cols, shift_rows[:, None], 0.0)
    )
    precond_rows = (
        shift_rows
        + jnp.einsum("pg,pg->g", left_all, left_all, preferred_element_type=jnp.float32)
        / norm_scale
    )
    picked = left_all[resident_ids].astype(jnp.float32) / factor[resident_ids][:, None]
    source_rows = picked.T
    col_ratio = col_count // row_count
    root_row = col_index // col_ratio
    source_cols, precond_cols = (
        from_root(source_rows, "row", root_row),
        from_root(precond_rows, "row", root_row),
    )
    screen_rows = source_rows / precond_rows[:, None]
    screen_cols = source_cols / precond_cols[:, None]
    for sweep_index in range(SWEEPS):
        last_sweep = sweep_index + 1 == SWEEPS
        row_image = lax.psum(
            jnp.dot(dielectric, screen_cols, precision=lax.Precision.HIGHEST), "col"
        )
        if not last_sweep:
            transposed = lax.dot_general(
                dielectric, screen_rows, (((0,), (0,)), ((), ())), precision=lax.Precision.HIGHEST
            )
            col_image = lax.psum(transposed, "row")
            screen_cols = screen_cols + damping * (source_cols - col_image) / precond_cols[:, None]
        screen_rows = screen_rows + damping * (source_rows - row_image) / precond_rows[:, None]
    partial_value = jnp.dot(
        pair_density.astype(jnp.float32), screen_rows, precision=lax.Precision.HIGHEST
    )
    summed = lax.psum_scatter(partial_value, "row", scatter_dimension=0, tiled=True)
    kernel_share = pair_dev // row_count
    weights = lax.dynamic_slice_in_dim(
        pair_weight, col_index * pair_dev + row_index * kernel_share, kernel_share
    ).astype(jnp.float32)
    kernel = weights[:, None] * summed / math.sqrt(NG)
    return (dielectric, kernel)


def solution(mesh):
    return jax.shard_map(
        shards,
        mesh=mesh,
        in_specs=(P("col", "row"), P(), P(), P(), P(), P("row", "col")),
        out_specs=(P("row", "col"), P(("col", "row"), None)),
        check_vma=False,
    )
```

profile of v0, /device:TPU:8, one launch (start us, length us, event | category | flops | bytes accessed | tf_op | source)
XLA Modules:
  0.0 609.8 jit_solution(10730562653668243322)
XLA Ops:
  7.2 0.0 all-gather.5.cloned.1.call-start
  7.2 0.7 select_select_fusion
  7.9 0.1 dynamic_slice.9
  8.0 1.8 multiply_convert_fusion
  9.8 0.0 all-gather.3.cloned.1.call-start
  9.8 0.7 all-gather.3.cloned.1.call-update
  10.6 42.7 %all-gather.5.cloned.1.call-done = bf16[256,8192]{1,0:T(8,128)(2,1)} async-done(((bf16[256,512]{1,0:T(8,128)(2,1)}), bf16[256,8192]{1,0:T(8,128)(2,1)}) %all-gather.5.cloned.1.call-update) | async-done | bytes 4194320 | tf_op jit(solution)/shard_map/all_gather | solution.py:40
  53.2 4.6 copy.26
  57.8 9.7 %all-to-all-start = ((bf16[256,16,512]{2,0,1:T(8,128)(2,1)}), bf16[256,16,512]{2,0,1:T(8,128)(2,1)}, u32[]{:S(2)}, u32[]{:S(2)}) async-start(bf16[256,16,512]{2,0,1:T(8,128)(2,1)} %bitcast.31), calls=%async_computation | async-start | bytes 8388608 | tf_op jit(solution)/shard_map/all_to_all | solution.py:41
  67.6 0.0 all-reduce.7.cloned.1.call-start
  67.7 3.1 gather_fusion.1
  70.8 132.1 %all-gather.3.cloned.1.call-done = bf16[4096,512]{1,0:T(8,128)(2,1)} async-done(((bf16[256,512]{1,0:T(8,128)(2,1)}), bf16[4096,512]{1,0:T(8,128)(2,1)}) %all-gather.3.cloned.1.call-update) | async-done | bytes 4194320 | tf_op jit(solution)/shard_map/all_gather | solution.py:39
  202.9 4.7 gather_fusion
  207.6 0.2 copy.14
  207.9 3.2 fusion
  211.1 0.8 broadcast_select_fusion
  211.8 1.2 fusion.16
  213.1 5.8 fusion.2
  218.9 3.2 fusion.17
  222.1 0.0 all-reduce.5.cloned.1.call-start
  222.2 31.7 %psum.36 = f32[512]{0:T(512)S(1)} all-reduce(f32[512]{0:T(512)S(1)} %get-tuple-element.12), channel_id=1, replica_groups=mesh['row'=16,'col'=16] {'row'}, use_global_device_ids=true, to_apply=%region_1.2 | all-reduce | flops 512 | bytes 4096 | tf_op jit(solution)/shard_map/psum | solution.py:14
  253.9 95.1 %all-reduce.7.cloned.1.call-done = (f32[512,512]{1,0:T(8,128)}, f32[512,512]{1,0:T(8,128)}) async-done(((f32[512,512]{1,0:T(8,128)}, f32[512,512]{1,0:T(8,128)}), (f32[512,512]{1,0:T(8,128)}, f32[512,512]{1,0:T(8,128)})) %all-reduce.7.cloned.1.call-update) | async-done | bytes 2097168 | tf_op jit(solution)/shard_map/psum | solution.py:14
  348.9 4.3 fusion.21
  353.3 3.1 fusion.7
  356.4 0.0 reduce-scatter.4.cloned.1.call-start
  356.5 177.0 %all-reduce.5.cloned.1.call-done = (f32[512,512]{1,0:T(8,128)}, f32[512,512]{1,0:T(8,128)}) async-done(((f32[512,512]{1,0:T(8,128)}, f32[512,512]{1,0:T(8,128)}), (f32[512,512]{1,0:T(8,128)}, f32[512,512]{1,0:T(8,128)})) %all-reduce.5.cloned.1.call-update) | async-done | bytes 2097168 | tf_op jit(solution)/shard_map/psum | solution.py:69
  533.5 2.9 convolution_bitcast_fusion
  536.4 1.0 copy.22
  537.4 0.8 dynamic-slice_convert_fusion
  538.2 63.4 %reduce-scatter.4.cloned.1.call-done = f32[16,512]{1,0:T(8,128)} async-done(((f32[256,512]{1,0:T(8,128)}), f32[16,512]{1,0:T(8,128)}) %reduce-scatter.4.cloned.1.call-update) | async-done | bytes 32784
  601.6 0.9 copy.23
  602.5 0.7 copy.15
  (21 shorter events, 0.1 us)
Async XLA Ops:
  7.2 46.1 %all-gather.5.cloned.1.call-start = ((), (), s32[]{:S(2)}) async-start(), calls=%async_computation.3 | async-start | bytes 4456448 | tf_op jit(solution)/shard_map/all_gather | solution.py:40
  9.8 193.1 %all-gather.3.cloned.1.call-start = ((), (), s32[]{:S(2)}) async-start(), calls=%async_computation.2 | async-start | bytes 4456448 | tf_op jit(solution)/shard_map/all_gather | solution.py:39
  57.8 9.8 %copy-start.1 = (s32[512]{0:T(512)S(1)}, s32[512]{0:T(512)}, u32[]{:S(2)}) copy-start(s32[512]{0:T(512)} %param.9) | copy-start | bytes 6148
  57.8 155.2 %all-to-all-start = ((bf16[256,16,512]{2,0,1:T(8,128)(2,1)}), bf16[256,16,512]{2,0,1:T(8,128)(2,1)}, u32[]{:S(2)}, u32[]{:S(2)}) async-start(bf16[256,16,512]{2,0,1:T(8,128)(2,1)} %bitcast.31), calls=%async_computation | async-start | bytes 8388608 | tf_op jit(solution)/shard_map/all_to_all | solution.py:41
  67.6 281.4 %all-reduce.7.cloned.1.call-start = ((), (), s32[]{:S(2)}) async-start(), calls=%async_computation.6 | async-start | bytes 4194304 | tf_op jit(solution)/shard_map/psum | solution.py:14
  207.6 5.4 copy-start.2
  218.9 134.4 %copy-start.5 = (f32[512,512]{1,0:T(8,128)}, f32[512,512]{1,0:T(8,128)S(1)}, u32[]{:S(2)}) copy-start(f32[512,512]{1,0:T(8,128)S(1)} %fusion.2) | copy-start | bytes 3145732
  222.1 311.4 %all-reduce.5.cloned.1.call-start = ((), (), s32[]{:S(2)}) async-start(), calls=%async_computation.5 | async-start | bytes 4194304 | tf_op jit(solution)/shard_map/psum | solution.py:69
  348.9 4.4 copy-start.3
  348.9 4.4 copy-start.4
  353.3 180.2 %copy-start = (bf16[256,512]{1,0:T(8,128)(2,1)S(1)}, bf16[256,512]{1,0:T(8,128)(2,1)}, u32[]{:S(2)}) copy-start(bf16[256,512]{1,0:T(8,128)(2,1)} %param.6) | copy-start | bytes 786436
  356.4 245.2 %reduce-scatter.4.cloned.1.call-start = ((), (), s32[]{:S(2)}) async-start(), calls=%async_computation.4 | async-start | bytes 557056
Sparse Core Ops, SparseCore 0:
  10.4 42.7 all-gather.4
  56.2 146.6 all-gather.2
  222.3 126.6 all-reduce.6
  356.5 176.8 all-reduce.4
  537.5 64.0 reduce-scatter.3
where the time goes:
time: 610 us
  waiting for transfers between devices  511 us (84%)
  blocking collectives  31.7 us (5%)
  matrix products  19.4 us (3%)
  local copies, waits for them, and re-layouts  15.4 us (3%)
  between operations  13.9 us (2%)
  starting transfers between devices  9.95 us (2%)
  other arithmetic  8.49 us (1%)
    psum x1, waiting for transfers between devices, shards(): lax.psum(jnp.dot(dielectric, screen_cols, precision=lax.Precision.HIGHEST...  177 us
    all_gather x1, waiting for transfers between devices, shards(): left_all = lax.all_gather(scaled, 'col', axis=0, tiled=True)  132 us
    psum x1, waiting for transfers between devices, from_root(): return lax.psum(block, axis)  95.1 us
    unnamed x6, waiting for transfers between devices  64.2 us
    all_gather x1, waiting for transfers between devices, shards(): pair_rows_all = lax.all_gather(scaled, 'row', axis=1, tiled=True)  42.7 us
    psum x1, blocking collectives, from_root(): return lax.psum(block, axis)  31.7 us
  transfers between devices with their start and end apart: 6, of which 5 were waited for; matrix products, arithmetic and copies ran while one was open for 3% of the time, Pallas kernels for 0%

commit v1 on v0

--- a/solution.py
+++ b/solution.py
@@ -9,9 +9,15 @@
 damping = 0.5
 
 
+def summed_here(x, name):
+    pieces = lax.all_gather(x, name, axis=0, tiled=False)
+    total = pieces.sum(axis=0)
+    return total
+
+
 def from_root(block, axis, owner):
     block = jnp.where(lax.axis_index(axis) == owner, block, jnp.zeros_like(block))
-    return lax.psum(block, axis)
+    return summed_here(block, axis)
 
 
 def scale_factor(exponent):

time: 610 us -> 703 us (1.15)
  waiting for transfers between devices: 511 us -> 608 us
  blocking collectives: 31.7 us -> 18.2 us
  other arithmetic: 8.49 us -> 17.1 us
    all_to_all x1, waiting for transfers between devices: 0.01 us -> 137 us  [shards(): lax.all_to_all(pair_rows_all, 'col', split_axis=1, concat_axis=0, tiled=T...]
    all_gather x1, waiting for transfers between devices: 132 us -> 75.4 us  [shards(): left_all = lax.all_gather(scaled, 'col', axis=0, tiled=True)]
    psum x1 -> x0, blocking collectives: 31.7 us -> none  [from_root(): return lax.psum(block, axis)]
    psum x1, waiting for transfers between devices: 95.1 us -> 115 us  [shards(): col_image = lax.psum(transposed, 'row')]
    all_gather x0 -> x1, blocking collectives: none -> 18.2 us  [summed_here(): pieces = lax.all_gather(x, name, axis=0, tiled=False)]
    reduce_sum x0 -> x2, other arithmetic: none -> 7.96 us  [summed_here(): total = pieces.sum(axis=0)]
    unnamed x6 -> x7, waiting for transfers between devices: 64.2 us -> 64.2 us
  transfers between devices with their start and end apart: 6 -> 7, of which waited for: 5 -> 7; matrix products, arithmetic and copies ran while one was open for 3% -> 6% of each run, Pallas kernels for 0% -> 0%
where the time goes in v1:
time: 703 us
  waiting for transfers between devices  608 us (86%)
  matrix products  19.4 us (3%)
  blocking collectives  18.2 us (3%)
  other arithmetic  17.1 us (2%)
  local copies, waits for them, and re-layouts  15.4 us (2%)
  between operations  14.2 us (2%)
  starting transfers between devices  9.86 us (1%)
    psum x1, waiting for transfers between devices, shards(): lax.psum(jnp.dot(dielectric, screen_cols, precision=lax.Precision.HIGHEST...  178 us
    all_to_all x1, waiting for transfers between devices, shards(): lax.all_to_all(pair_rows_all, 'col', split_axis=1, concat_axis=0, tiled=T...  137 us
    psum x1, waiting for transfers between devices, shards(): col_image = lax.psum(transposed, 'row')  115 us
    all_gather x1, waiting for transfers between devices, shards(): left_all = lax.all_gather(scaled, 'col', axis=0, tiled=True)  75.4 us
    unnamed x7, waiting for transfers between devices  64.2 us
    all_gather x1, waiting for transfers between devices, shards(): pair_rows_all = lax.all_gather(scaled, 'row', axis=1, tiled=True)  36 us
    all_gather x1, blocking collectives, summed_here(): pieces = lax.all_gather(x, name, axis=0, tiled=False)  18.2 us
  transfers between devices with their start and end apart: 7, of which 7 were waited for; matrix products, arithmetic and copies ran while one was open for 6% of the time, Pallas kernels for 0%

profile of v1, /device:TPU:8, one launch (start us, length us, event | category | flops | bytes accessed | tf_op | source)
XLA Modules:
  0.0 702.6 jit_solution(9417552925331624193)
XLA Ops:
  7.2 0.7 select_select_fusion
  7.9 0.1 dynamic_slice.9
  8.0 1.8 multiply_convert_fusion
  9.8 0.7 all-gather.9.cloned.1.call-update
  10.6 0.7 compare_select_fusion
  11.3 3.1 gather_fusion.1
  14.4 75.4 %all-gather.7.cloned.1.call-done = bf16[4096,512]{1,0:T(8,128)(2,1)} async-done(((bf16[256,512]{1,0:T(8,128)(2,1)}), bf16[4096,512]{1,0:T(8,128)(2,1)}) %all-gather.7.cloned.1.call-update) | async-done | bytes 4194320 | tf_op jit(solution)/shard_map/all_gather | solution.py:45
  89.8 4.7 gather_fusion
  94.6 0.2 copy.14
  94.8 1.2 fusion.16
  96.0 36.0 %all-gather.9.cloned.1.call-done = bf16[256,8192]{1,0:T(8,128)(2,1)} async-done(((bf16[256,512]{1,0:T(8,128)(2,1)}), bf16[256,8192]{1,0:T(8,128)(2,1)}) %all-gather.9.cloned.1.call-update) | async-done | bytes 4194320 | tf_op jit(solution)/shard_map/all_gather | solution.py:46
  132.0 4.6 copy.26
  136.6 9.6 %all-to-all-start = ((bf16[256,16,512]{2,0,1:T(8,128)(2,1)}), bf16[256,16,512]{2,0,1:T(8,128)(2,1)}, u32[]{:S(2)}, u32[]{:S(2)}) async-start(bf16[256,16,512]{2,0,1:T(8,128)(2,1)} %bitcast.34), calls=%async_computation | async-start | bytes 8388608 | tf_op jit(solution)/shard_map/all_to_all | solution.py:47
  146.2 0.0 all-reduce.4.cloned.1.call-start
  146.3 3.2 fusion
  149.5 0.8 broadcast_select_fusion
  150.3 136.9 %all-to-all-done = bf16[256,16,512]{2,0,1:T(8,128)(2,1)} async-done(((bf16[256,16,512]{2,0,1:T(8,128)(2,1)}), bf16[256,16,512]{2,0,1:T(8,128)(2,1)}, u32[]{:S(2)}, u32[]{:S(2)}) %all-to-all-start) | async-done | bytes 4194336 | tf_op jit(solution)/shard_map/all_to_all | solution.py:47
  287.2 6.0 fusion.2
  293.2 3.2 fusion.17
  296.5 18.2 %all-gather.2 = f32[16,1,512]{2,1,0:T(1,128)S(1)} all-gather(f32[1,1,512]{2,1,0:T(1,128)S(1)} %bitcast.36), channel_id=3, replica_groups=mesh['row'=16,'col'=16] {'row'}, dimensions={0}, use_global_device_ids=true | all-gather | bytes 34816 | tf_op jit(solution)/shard_map/all_gather | solution.py:13
  314.7 3.3 all-gather.11.cloned.1.call-done
  318.1 7.9 %reduce_sum.18 = f32[512,512]{1,0:T(8,128)S(1)} reduce(f32[16,512,512]{2,1,0:T(8,128)} %bitcast.33, f32[]{:T(128)} %constant.49.clone.1), dimensions={0}, to_apply=%region_0.1 | reduce | flops 3932160 | bytes 17825796 | tf_op jit(solution)/shard_map/reduce_sum | solution.py:14
  326.0 2.9 fusion.21
  329.0 115.1 %all-reduce.4.cloned.1.call-done = f32[512,512]{1,0:T(8,128)} async-done(((f32[512,512]{1,0:T(8,128)}), f32[512,512]{1,0:T(8,128)}) %all-reduce.4.cloned.1.call-update) | async-done | bytes 1048592 | tf_op jit(solution)/shard_map/psum | solution.py:82
  444.0 4.3 fusion.7
  448.5 177.5 %all-reduce.6.cloned.1.call-done = (f32[512,512]{1,0:T(8,128)}, f32[512,512]{1,0:T(8,128)}) async-done(((f32[512,512]{1,0:T(8,128)}, f32[512,512]{1,0:T(8,128)}), (f32[512,512]{1,0:T(8,128)}, f32[512,512]{1,0:T(8,128)})) %all-reduce.6.cloned.1.call-update) | async-done | bytes 2097168 | tf_op jit(solution)/shard_map/psum | solution.py:75
  626.0 2.9 convolution_bitcast_fusion
  628.9 1.0 copy.22
  629.9 0.8 dynamic-slice_convert_fusion
  630.7 63.4 %reduce-scatter.4.cloned.1.call-done = f32[16,512]{1,0:T(8,128)} async-done(((f32[256,512]{1,0:T(8,128)}), f32[16,512]{1,0:T(8,128)}) %reduce-scatter.4.cloned.1.call-update) | async-done | bytes 32784
  694.1 0.9 copy.23
  695.1 0.7 copy.15
  (20 shorter events, 0.4 us)
Async XLA Ops:
  7.2 82.7 %all-gather.7.cloned.1.call-start = ((), (), s32[]{:S(2)}) async-start(), calls=%async_computation.2 | async-start | bytes 4456448 | tf_op jit(solution)/shard_map/all_gather | solution.py:45
  9.8 122.2 %all-gather.9.cloned.1.call-start = ((), (), s32[]{:S(2)}) async-start(), calls=%async_computation.3 | async-start | bytes 4456448 | tf_op jit(solution)/shard_map/all_gather | solution.py:46
  10.6 307.5 %all-gather.11.cloned.1.call-start = ((), (), s32[]{:S(2)}) async-start(), calls=%async_computation.5 | async-start | bytes 17825792 | tf_op jit(solution)/shard_map/all_gather | solution.py:13
  136.6 150.6 %all-to-all-start = ((bf16[256,16,512]{2,0,1:T(8,128)(2,1)}), bf16[256,16,512]{2,0,1:T(8,128)(2,1)}, u32[]{:S(2)}, u32[]{:S(2)}) async-start(bf16[256,16,512]{2,0,1:T(8,128)(2,1)} %bitcast.34), calls=%async_computation | async-start | bytes 8388608 | tf_op jit(solution)/shard_map/all_to_all | solution.py:47
  146.2 140.9 %copy-start.1 = (f32[512,512]{1,0:T(8,128)S(1)}, f32[512,512]{1,0:T(8,128)}, u32[]{:S(2)}) copy-start(f32[512,512]{1,0:T(8,128)} %param.11) | copy-start | bytes 3145732
  146.2 297.8 %all-reduce.4.cloned.1.call-start = ((), (), s32[]{:S(2)}) async-start(), calls=%async_computation.4 | async-start | bytes 2097152 | tf_op jit(solution)/shard_map/psum | solution.py:82
  293.2 150.9 %copy-start.2 = (f32[512,512]{1,0:T(8,128)}, f32[512,512]{1,0:T(8,128)S(1)}, u32[]{:S(2)}) copy-start(f32[512,512]{1,0:T(8,128)S(1)} %fusion.2) | copy-start | bytes 3145732
  296.5 329.6 %all-reduce.6.cloned.1.call-start = ((), (), s32[]{:S(2)}) async-start(), calls=%async_computation.7 | async-start | bytes 4194304 | tf_op jit(solution)/shard_map/psum | solution.py:75
  328.9 297.1 %copy-start = (bf16[256,512]{1,0:T(8,128)(2,1)S(1)}, bf16[256,512]{1,0:T(8,128)(2,1)}, u32[]{:S(2)}) copy-start(bf16[256,512]{1,0:T(8,128)(2,1)} %param.6) | copy-start | bytes 786436
  448.4 245.7 %reduce-scatter.4.cloned.1.call-start = ((), (), s32[]{:S(2)}) async-start(), calls=%async_computation.6 | async-start | bytes 557056
Sparse Core Ops, SparseCore 0:
  11.0 78.7 all-gather.6
  92.2 39.7 all-gather.8
  133.8 184.1 all-gather.10
  320.6 123.4 all-reduce.3
  448.5 177.4 all-reduce.5
  630.1 64.0 reduce-scatter.3
